TPU v7x, 32 devices: a whole 2x2x4 slice. The times are simulated.
32 devices in a mesh: row: 8 (over z, y), col: 4 (over x, core).
Axes of the slice: x: 2, y: 2, z: 4, core: 2. Of those that a mesh axis runs over, the one named last changes fastest.
Arguments:
- bands: float32 [13, 256, 512], P(None, 'row', 'col'), may hold values from -6 to 6
- kern_small: float32 [13, 5, 5], replicated, may hold values from -1.25 to 1.25
- kern_large: float32 [13, 9, 9], replicated, may hold values from -0.625 to 0.625
- mix_weight: float32 [39, 64], replicated, may hold values from -2.4 to 2.4
- node_ids: int32 [256, 512], P('row', 'col'), may hold values from 0 to 1
- labels: int32 [256, 512], P('row', 'col'), may hold values from 0 to 39
- edges: int32 [64, 256], replicated, may hold values from -7000 to 13104, as said below
Outputs:
- hist: float32 [64, 2, 40, 256], P('row', None, None, 'col')
Inputs may be any that keep to these rules, and one draw needn't show every extreme that they name: `edges`: strictly increasing along the bins.
All inputs are finite; a program needn't handle non-finite values.
Results may differ from a plain program's by a relative error of at most 0.0003.
Values sent between devices are 32-bit elements; how exact they have to be, the bound alone decides.
A program may use at most 128 MiB of HBM per device.

v0:
```python
import jax
import jax.numpy as jnp
from jax import lax
from jax.sharding import PartitionSpec as P

FEAT = 64
BINS = 256
CLASSES = 40
NODES = 2


def with_halo(block, sides, width):
    for axis, dim in sides:
        count = lax.axis_size(axis)
        forward = [(i, i + 1) for i in range(count - 1)]
        backward = [(target, source) for source, target in forward]
        low = lax.ppermute(
            lax.slice_in_dim(block, block.shape[dim] - width, None, axis=dim), axis, forward
        )
        high = lax.ppermute(lax.slice_in_dim(block, 0, width, axis=dim), axis, backward)
        block = jnp.concatenate([low, block, high], axis=dim)
    return block


def stencil(padded, kernel, margin, tile_height, tile_width):
    reach = (kernel.shape[1] - 1) // 2
    running = jnp.zeros((padded.shape[0], tile_height, tile_width), jnp.float32)
    for row_off in range(kernel.shape[1]):
        for col_off in range(kernel.shape[2]):
            first_row = margin - reach + row_off
            first_col = margin - reach + col_off
            window = padded[
                :, first_row : first_row + tile_height, first_col : first_col + tile_width
            ]
            running = running + kernel[:, row_off, col_off][:, None, None] * window
    return running


def tent_weights(values, centres):
    clamped = jnp.clip(values, centres[:, :1], centres[:, -1:])
    bin_gaps = centres[:, 1:] - centres[:, :-1]
    rising = (clamped[:, None, :] - centres[:, :-1, None]) / bin_gaps[:, :, None]
    falling = (centres[:, 1:, None] - clamped[:, None, :]) / bin_gaps[:, :, None]
    unit_row = jnp.ones((values.shape[0], 1, values.shape[1]), jnp.float32)
    rising_full = jnp.concatenate([unit_row, rising], axis=1)
    falling_full = jnp.concatenate([falling, unit_row], axis=1)
    return jnp.clip(jnp.minimum(rising_full, falling_full), 0.0, 1.0).astype(jnp.bfloat16)


def body(bands, kern_small, kern_large, mix_weight, node_ids, labels, edges):
    band_count, tile_height, tile_width = bands.shape
    padded_near = with_halo(bands, (("row", 1), ("col", 2)), 2)
    padded_far = with_halo(bands, (("row", 1), ("col", 2)), 4)
    small_field = stencil(padded_near, kern_small, 2, tile_height, tile_width)
    large_field = stencil(padded_far, kern_large, 4, tile_height, tile_width)
    pixels = tile_height * tile_width
    stacked = jnp.concatenate([bands, small_field, large_field], axis=0).reshape(
        3 * band_count, pixels
    )
    features = jnp.dot(
        mix_weight.T, stacked, precision=lax.Precision.HIGHEST, preferred_element_type=jnp.float32
    )
    centres_all = edges.astype(jnp.float32) / 1024.0
    cell_code = node_ids.reshape(pixels) * CLASSES + labels.reshape(pixels)
    pair_count = NODES * CLASSES
    one_hot = (cell_code[None, :] == jnp.arange(pair_count, dtype=jnp.int32)[:, None]).astype(
        jnp.bfloat16
    )
    block_rows = min(512, pixels)
    block_count = pixels // block_rows
    hot_blocks = one_hot.reshape(pair_count, block_count, block_rows).transpose(1, 0, 2)
    row_devices = lax.axis_size("row")
    col_devices = lax.axis_size("col")
    feature_share = FEAT // row_devices
    bin_share = BINS // col_devices
    value_blocks = features.reshape(FEAT, block_count, block_rows).transpose(1, 0, 2)

    def accumulate(running, pair):
        block_values, block_hot = pair
        weights = tent_weights(block_values, centres_all)
        product = jnp.einsum("kp,fbp->fkb", block_hot, weights, preferred_element_type=jnp.float32)
        return (running + product, None)

    start_sum = jnp.zeros((FEAT, pair_count, BINS), jnp.float32)
    running, unused = lax.scan(accumulate, start_sum, (value_blocks, hot_blocks))
    whole_term = running.reshape(FEAT, NODES, CLASSES, BINS)
    ordered = whole_term.reshape(row_devices, feature_share, NODES, CLASSES, col_devices, bin_share)
    ordered = ordered.transpose(0, 4, 1, 2, 3, 5).reshape(
        row_devices * col_devices * feature_share, NODES, CLASSES, bin_share
    )
    summed = lax.psum_scatter(ordered, ("row", "col"), scatter_dimension=0, tiled=True)
    scale = float(NODES * CLASSES * BINS) / float(pixels * row_devices * col_devices)
    return summed * scale


def solution(mesh):
    return jax.shard_map(
        body,
        mesh=mesh,
        in_specs=(P(None, "row", "col"), P(), P(), P(), P("row", "col"), P("row", "col"), P()),
        out_specs=P("row", None, None, "col"),
        check_vma=False,
    )
```

profile of v0, /device:TPU:0, one launch (start us, length us, event | category | flops | bytes accessed | tf_op | source)
XLA Modules:
  0.0 492.7 jit_solution(17593657151220061317)
XLA Ops:
  6.5 0.9 fusion.126
  7.4 4.9 collective-permute-start.4
  12.3 1.3 collective-permute-start.5
  13.6 0.9 fusion.125
  14.5 4.5 collective-permute-start
  19.0 1.3 collective-permute-start.1
  20.3 1.6 slice_reduce_fusion.79
  21.9 1.8 slice_reduce_fusion.78
  23.7 1.6 slice_reduce_fusion.77
  25.3 1.7 slice_reduce_fusion.80
  27.0 1.0 constant_dynamic-update-slice_fusion.1
  28.0 0.9 slice_bitcast_fusion.26
  28.9 0.8 slice_bitcast_fusion.25
  29.7 0.9 copy.17
  30.7 0.7 multiply_add_fusion
  31.5 0.2 fusion.7
  31.7 1.1 slice_reduce_fusion.76
  32.8 0.1 copy.23
  32.9 1.0 pad_maximum_fusion.3
  33.9 0.1 fusion.123
  34.1 1.3 collective-permute-start.2
  35.4 1.3 collective-permute-start.3
  36.7 3.8 collective-permute-done.3
  40.5 1.3 maximum_maximum_fusion
  41.8 2.5 fusion.119
  44.4 1.0 pad_maximum_fusion.4
  45.3 0.1 fusion.124
  45.5 6.7 %collective-permute-start.6 = (f32[13,40,4]{2,1,0:T(8,128)S(1)}, f32[13,40,4]{2,1,0:T(8,128)S(1)}, u32[]{:S(2)}, u32[]{:S(2)}) collective-permute-start(f32[13,40,4]{2,1,0:T(8,128)S(1)} %get-tuple-element.182), channel_id=1, source_target_pairs={{0,1},{1,2},{2,3},{4,5},{5,6},{6,7},{8,9},{9,10},{10,11},{12,13},{... | collective-permute-start | bytes 24968 | tf_op jit(solution)/shard_map/ppermute | solution.py:17
  52.2 1.5 collective-permute-start.7
  53.7 1.9 collective-permute-done.7
  55.6 1.3 maximum_maximum_fusion.1
  56.9 7.2 %fusion.78 = f32[13,32,128]{2,1,0:T(8,128)S(1)} fusion(f32[13,40,132]{2,1,0:T(8,128)S(1)} %get-tuple-element.181, f32[13,36,128]{2,1,0:T(8,128)S(1)} %constant_dynamic-update-slice_fusion.2, f32[13,40,132]{2,1,0:T(8,128)S(1)} %get-tuple-element.180, f32[13,32,128]{2,1,0:T(8,128)} %param.9, f32[13,4,128]{2,1,0:T(4,128)S(1)} %collective-permute-done.4, ...), kind=kLoop, calls=%fused_computation.103 | loop fusion | flops 8785920 | bytes 16644212 | tf_op jit(solution)/shard_map/add | solution.py:35
  64.2 0.4 copy.25
  64.6 1.0 fusion.128
  65.7 0.1 copy.27
  65.8 239.9 %while.12 = (s32[]{:T(128)}, f32[64,80,256]{2,1,0:T(8,128)}, f32[64,256]{0,1:T(8,128)S(1)}, f32[8,64,512]{2,1,0:T(8,128)S(1)}, f32[64,255]{1,0:T(8,128)S(1)}, /*...) while((s32[]{:T(128)}, f32[64,80,256]{2,1,0:T(8,128)}, f32[64,256]{0,1:T(8,128)S(1)}, ...), condition=%wide.region_1.2_spmd.clone, body=%wide.region_0.1_spmd.clone.sunk | while | flops 1436942336 | bytes 78527336 | solution.py:85
  65.8 0.1 fusion.136
  66.1 11.5 %subtract_divide_fusion.3 = (bf16[64,255,512]{2,1,0:T(8,128)(2,1)}, bf16[64,255,512]{2,1,0:T(8,128)(2,1)}) fusion(f32[64,255]{1,0:T(8,128)S(1)} %get-tuple-element.288, f32[64,255]{1,0:T(8,128)S(1)} %copy.30, f32[64,512]{1,0:T(8,128)S(1)} %fusion.136, f32[64,255]{1,0:T(8,128)S(1)} %copy.31), kind=kLoop, calls=%fused_computation.2.clone.1 | loop fusion | flops 50135040 | bytes 33750272 | tf_op jit(solution)/shard_map/while/body/eval_jaxpr/div | solution.py:42
  77.6 16.3 %bitcast_add_fusion.2 = f32[64,80,256]{2,1,0:T(8,128)} fusion(f32[64,80,256]{2,1,0:T(8,128)} %get-tuple-element.277, pred[]{:T(512)S(6)} %compare.5, bf16[64,255,512]{2,1,0:T(8,128)(2,1)} %get-tuple-element.266, bf16[64,255,512]{2,1,0:T(8,128)(2,1)} %get-tuple-element.267, bf16[8,80,512]{2,1,0:T(8,128)(2,1)S(1)} %get-tuple-element.289, ...), kind=kOutput, calls=%fused_computation.4.clone.1 | convolution fusion | flops 1386741760 | bytes 43991044 | tf_op jit(solution)/shard_map/while/body/eval_jaxpr/kp,fbp->fkb/dot_general | solution.py:81
  93.9 0.1 fusion.136
  94.2 11.5 %subtract_divide_fusion.3 = (bf16[64,255,512]{2,1,0:T(8,128)(2,1)}, bf16[64,255,512]{2,1,0:T(8,128)(2,1)}) fusion(f32[64,255]{1,0:T(8,128)S(1)} %get-tuple-element.288, f32[64,255]{1,0:T(8,128)S(1)} %copy.30, f32[64,512]{1,0:T(8,128)S(1)} %fusion.136, f32[64,255]{1,0:T(8,128)S(1)} %copy.31), kind=kLoop, calls=%fused_computation.2.clone.1 | loop fusion | flops 50135040 | bytes 33750272 | tf_op jit(solution)/shard_map/while/body/eval_jaxpr/div | solution.py:42
  105.7 18.5 %bitcast_add_fusion.2 = f32[64,80,256]{2,1,0:T(8,128)} fusion(f32[64,80,256]{2,1,0:T(8,128)} %get-tuple-element.277, pred[]{:T(512)S(6)} %compare.5, bf16[64,255,512]{2,1,0:T(8,128)(2,1)} %get-tuple-element.266, bf16[64,255,512]{2,1,0:T(8,128)(2,1)} %get-tuple-element.267, bf16[8,80,512]{2,1,0:T(8,128)(2,1)S(1)} %get-tuple-element.289, ...), kind=kOutput, calls=%fused_computation.4.clone.1 | convolution fusion | flops 1386741760 | bytes 43991044 | tf_op jit(solution)/shard_map/while/body/eval_jaxpr/kp,fbp->fkb/dot_general | solution.py:81
  124.2 0.1 fusion.136
  124.4 11.5 %subtract_divide_fusion.3 = (bf16[64,255,512]{2,1,0:T(8,128)(2,1)}, bf16[64,255,512]{2,1,0:T(8,128)(2,1)}) fusion(f32[64,255]{1,0:T(8,128)S(1)} %get-tuple-element.288, f32[64,255]{1,0:T(8,128)S(1)} %copy.30, f32[64,512]{1,0:T(8,128)S(1)} %fusion.136, f32[64,255]{1,0:T(8,128)S(1)} %copy.31), kind=kLoop, calls=%fused_computation.2.clone.1 | loop fusion | flops 50135040 | bytes 33750272 | tf_op jit(solution)/shard_map/while/body/eval_jaxpr/div | solution.py:42
  135.9 18.5 %bitcast_add_fusion.2 = f32[64,80,256]{2,1,0:T(8,128)} fusion(f32[64,80,256]{2,1,0:T(8,128)} %get-tuple-element.277, pred[]{:T(512)S(6)} %compare.5, bf16[64,255,512]{2,1,0:T(8,128)(2,1)} %get-tuple-element.266, bf16[64,255,512]{2,1,0:T(8,128)(2,1)} %get-tuple-element.267, bf16[8,80,512]{2,1,0:T(8,128)(2,1)S(1)} %get-tuple-element.289, ...), kind=kOutput, calls=%fused_computation.4.clone.1 | convolution fusion | flops 1386741760 | bytes 43991044 | tf_op jit(solution)/shard_map/while/body/eval_jaxpr/kp,fbp->fkb/dot_general | solution.py:81
  154.4 0.1 fusion.136
  154.7 11.5 %subtract_divide_fusion.3 = (bf16[64,255,512]{2,1,0:T(8,128)(2,1)}, bf16[64,255,512]{2,1,0:T(8,128)(2,1)}) fusion(f32[64,255]{1,0:T(8,128)S(1)} %get-tuple-element.288, f32[64,255]{1,0:T(8,128)S(1)} %copy.30, f32[64,512]{1,0:T(8,128)S(1)} %fusion.136, f32[64,255]{1,0:T(8,128)S(1)} %copy.31), kind=kLoop, calls=%fused_computation.2.clone.1 | loop fusion | flops 50135040 | bytes 33750272 | tf_op jit(solution)/shard_map/while/body/eval_jaxpr/div | solution.py:42
  166.2 18.5 %bitcast_add_fusion.2 = f32[64,80,256]{2,1,0:T(8,128)} fusion(f32[64,80,256]{2,1,0:T(8,128)} %get-tuple-element.277, pred[]{:T(512)S(6)} %compare.5, bf16[64,255,512]{2,1,0:T(8,128)(2,1)} %get-tuple-element.266, bf16[64,255,512]{2,1,0:T(8,128)(2,1)} %get-tuple-element.267, bf16[8,80,512]{2,1,0:T(8,128)(2,1)S(1)} %get-tuple-element.289, ...), kind=kOutput, calls=%fused_computation.4.clone.1 | convolution fusion | flops 1386741760 | bytes 43991044 | tf_op jit(solution)/shard_map/while/body/eval_jaxpr/kp,fbp->fkb/dot_general | solution.py:81
  184.6 0.1 fusion.136
  184.9 11.5 %subtract_divide_fusion.3 = (bf16[64,255,512]{2,1,0:T(8,128)(2,1)}, bf16[64,255,512]{2,1,0:T(8,128)(2,1)}) fusion(f32[64,255]{1,0:T(8,128)S(1)} %get-tuple-element.288, f32[64,255]{1,0:T(8,128)S(1)} %copy.30, f32[64,512]{1,0:T(8,128)S(1)} %fusion.136, f32[64,255]{1,0:T(8,128)S(1)} %copy.31), kind=kLoop, calls=%fused_computation.2.clone.1 | loop fusion | flops 50135040 | bytes 33750272 | tf_op jit(solution)/shard_map/while/body/eval_jaxpr/div | solution.py:42
  196.4 18.5 %bitcast_add_fusion.2 = f32[64,80,256]{2,1,0:T(8,128)} fusion(f32[64,80,256]{2,1,0:T(8,128)} %get-tuple-element.277, pred[]{:T(512)S(6)} %compare.5, bf16[64,255,512]{2,1,0:T(8,128)(2,1)} %get-tuple-element.266, bf16[64,255,512]{2,1,0:T(8,128)(2,1)} %get-tuple-element.267, bf16[8,80,512]{2,1,0:T(8,128)(2,1)S(1)} %get-tuple-element.289, ...), kind=kOutput, calls=%fused_computation.4.clone.1 | convolution fusion | flops 1386741760 | bytes 43991044 | tf_op jit(solution)/shard_map/while/body/eval_jaxpr/kp,fbp->fkb/dot_general | solution.py:81
  214.9 0.1 fusion.136
  215.2 11.5 %subtract_divide_fusion.3 = (bf16[64,255,512]{2,1,0:T(8,128)(2,1)}, bf16[64,255,512]{2,1,0:T(8,128)(2,1)}) fusion(f32[64,255]{1,0:T(8,128)S(1)} %get-tuple-element.288, f32[64,255]{1,0:T(8,128)S(1)} %copy.30, f32[64,512]{1,0:T(8,128)S(1)} %fusion.136, f32[64,255]{1,0:T(8,128)S(1)} %copy.31), kind=kLoop, calls=%fused_computation.2.clone.1 | loop fusion | flops 50135040 | bytes 33750272 | tf_op jit(solution)/shard_map/while/body/eval_jaxpr/div | solution.py:42
  226.7 18.5 %bitcast_add_fusion.2 = f32[64,80,256]{2,1,0:T(8,128)} fusion(f32[64,80,256]{2,1,0:T(8,128)} %get-tuple-element.277, pred[]{:T(512)S(6)} %compare.5, bf16[64,255,512]{2,1,0:T(8,128)(2,1)} %get-tuple-element.266, bf16[64,255,512]{2,1,0:T(8,128)(2,1)} %get-tuple-element.267, bf16[8,80,512]{2,1,0:T(8,128)(2,1)S(1)} %get-tuple-element.289, ...), kind=kOutput, calls=%fused_computation.4.clone.1 | convolution fusion | flops 1386741760 | bytes 43991044 | tf_op jit(solution)/shard_map/while/body/eval_jaxpr/kp,fbp->fkb/dot_general | solution.py:81
  245.1 0.1 fusion.136
  245.4 11.5 %subtract_divide_fusion.3 = (bf16[64,255,512]{2,1,0:T(8,128)(2,1)}, bf16[64,255,512]{2,1,0:T(8,128)(2,1)}) fusion(f32[64,255]{1,0:T(8,128)S(1)} %get-tuple-element.288, f32[64,255]{1,0:T(8,128)S(1)} %copy.30, f32[64,512]{1,0:T(8,128)S(1)} %fusion.136, f32[64,255]{1,0:T(8,128)S(1)} %copy.31), kind=kLoop, calls=%fused_computation.2.clone.1 | loop fusion | flops 50135040 | bytes 33750272 | tf_op jit(solution)/shard_map/while/body/eval_jaxpr/div | solution.py:42
  256.9 18.5 %bitcast_add_fusion.2 = f32[64,80,256]{2,1,0:T(8,128)} fusion(f32[64,80,256]{2,1,0:T(8,128)} %get-tuple-element.277, pred[]{:T(512)S(6)} %compare.5, bf16[64,255,512]{2,1,0:T(8,128)(2,1)} %get-tuple-element.266, bf16[64,255,512]{2,1,0:T(8,128)(2,1)} %get-tuple-element.267, bf16[8,80,512]{2,1,0:T(8,128)(2,1)S(1)} %get-tuple-element.289, ...), kind=kOutput, calls=%fused_computation.4.clone.1 | convolution fusion | flops 1386741760 | bytes 43991044 | tf_op jit(solution)/shard_map/while/body/eval_jaxpr/kp,fbp->fkb/dot_general | solution.py:81
  275.4 0.1 fusion.136
  275.7 11.5 %subtract_divide_fusion.3 = (bf16[64,255,512]{2,1,0:T(8,128)(2,1)}, bf16[64,255,512]{2,1,0:T(8,128)(2,1)}) fusion(f32[64,255]{1,0:T(8,128)S(1)} %get-tuple-element.288, f32[64,255]{1,0:T(8,128)S(1)} %copy.30, f32[64,512]{1,0:T(8,128)S(1)} %fusion.136, f32[64,255]{1,0:T(8,128)S(1)} %copy.31), kind=kLoop, calls=%fused_computation.2.clone.1 | loop fusion | flops 50135040 | bytes 33750272 | tf_op jit(solution)/shard_map/while/body/eval_jaxpr/div | solution.py:42
  287.2 18.5 %bitcast_add_fusion.2 = f32[64,80,256]{2,1,0:T(8,128)} fusion(f32[64,80,256]{2,1,0:T(8,128)} %get-tuple-element.277, pred[]{:T(512)S(6)} %compare.5, bf16[64,255,512]{2,1,0:T(8,128)(2,1)} %get-tuple-element.266, bf16[64,255,512]{2,1,0:T(8,128)(2,1)} %get-tuple-element.267, bf16[8,80,512]{2,1,0:T(8,128)(2,1)S(1)} %get-tuple-element.289, ...), kind=kOutput, calls=%fused_computation.4.clone.1 | convolution fusion | flops 1386741760 | bytes 43991044 | tf_op jit(solution)/shard_map/while/body/eval_jaxpr/kp,fbp->fkb/dot_general | solution.py:81
  305.6 9.9 %reshape_reshape.3 = f32[8,8,2,40,4,64]{5,4,3,2,1,0:T(4,128)} reshape(f32[64,80,256]{2,1,0:T(8,128)} %get-tuple-element.57) | data formatting | bytes 10485760 | tf_op jit(solution)/shard_map/reshape;reshape | solution.py:87
  315.6 9.2 %copy.21 = f32[8,8,2,40,4,64]{5,3,2,1,4,0:T(8,128)} copy(f32[8,8,2,40,4,64]{5,4,3,2,1,0:T(4,128)} %reshape_reshape.3) | data formatting | bytes 10485760 | tf_op jit(solution)/shard_map/reshape;reshape | solution.py:87
  324.7 159.4 %reduce-scatter.2.cloned.1.call-done = f32[8,2,40,64]{3,2,1,0:T(8,128)} async-done(((f32[256,2,40,64]{3,2,1,0:T(8,128)}), f32[8,2,40,64]{3,2,1,0:T(8,128)}) %reduce-scatter.2.cloned.1.call-update) | async-done | bytes 163856 | tf_op jit(solution)/shard_map/reduce_scatter | solution.py:91
  484.1 1.7 broadcast_multiply_fusion
  (56 shorter events, 1.7 us)
Async XLA Ops:
  6.5 58.1 %copy-start = (f32[39,64]{1,0:T(8,128)S(1)}, f32[39,64]{1,0:T(8,128)}, u32[]{:S(2)}) copy-start(f32[39,64]{1,0:T(8,128)} %param.12) | copy-start | bytes 29956
  6.5 57.6 %copy-start.2 = (f32[13,32,128]{2,1,0:T(8,128)S(1)}, f32[13,32,128]{2,1,0:T(8,128)}, u32[]{:S(2)}) copy-start(f32[13,32,128]{2,1,0:T(8,128)} %param.9) | copy-start | bytes 638980
  6.5 477.6 %reduce-scatter.2.cloned.1.call-start = ((), (), s32[]{:S(2)}) async-start(), calls=%async_computation.1 | async-start | bytes 10813440 | tf_op jit(solution)/shard_map/reduce_scatter | solution.py:91
  7.4 36.9 %collective-permute-start.4 = (f32[13,4,128]{2,1,0:T(4,128)S(1)}, f32[13,4,128]{2,1,0:T(4,128)S(1)}, u32[]{:S(2)}, u32[]{:S(2)}) collective-permute-start(f32[13,4,128]{2,1,0:T(4,128)S(1)} %get-tuple-element.190), channel_id=1, source_target_pairs={{0,4},{4,8},{8,12},{12,16},{16,20},{20,24},{24,28},{1,5},{5,9},{9,... | collective-permute-start | bytes 79880 | tf_op jit(solution)/shard_map/ppermute | solution.py:17
  12.3 32.0 %collective-permute-start.5 = (f32[13,4,128]{2,1,0:T(4,128)S(1)}, f32[13,4,128]{2,1,0:T(4,128)S(1)}, u32[]{:S(2)}, u32[]{:S(2)}) collective-permute-start(f32[13,4,128]{2,1,0:T(4,128)S(1)} %get-tuple-element.191), channel_id=1, source_target_pairs={{4,0},{8,4},{12,8},{16,12},{20,16},{24,20},{28,24},{5,1},{9,5},{13... | collective-permute-start | bytes 79880 | tf_op jit(solution)/shard_map/ppermute | solution.py:20
  14.5 18.5 %collective-permute-start = (f32[13,2,128]{2,1,0:T(2,128)S(1)}, f32[13,2,128]{2,1,0:T(2,128)S(1)}, u32[]{:S(2)}, u32[]{:S(2)}) collective-permute-start(f32[13,2,128]{2,1,0:T(2,128)S(1)} %get-tuple-element.188), channel_id=1, source_target_pairs={{0,4},{4,8},{8,12},{12,16},{16,20},{20,24},{24,28},{1,5},{5,9},{9,... | collective-permute-start | bytes 39944 | tf_op jit(solution)/shard_map/ppermute | solution.py:17
  19.0 13.9 %collective-permute-start.1 = (f32[13,2,128]{2,1,0:T(2,128)S(1)}, f32[13,2,128]{2,1,0:T(2,128)S(1)}, u32[]{:S(2)}, u32[]{:S(2)}) collective-permute-start(f32[13,2,128]{2,1,0:T(2,128)S(1)} %get-tuple-element.189), channel_id=1, source_target_pairs={{4,0},{8,4},{12,8},{16,12},{20,16},{24,20},{28,24},{5,1},{9,5},{13... | collective-permute-start | bytes 39944 | tf_op jit(solution)/shard_map/ppermute | solution.py:20
  34.1 2.6 collective-permute-start.2
  35.4 5.1 %collective-permute-start.3 = (f32[13,36,2]{2,1,0:T(8,128)S(1)}, f32[13,36,2]{2,1,0:T(8,128)S(1)}, u32[]{:S(2)}, u32[]{:S(2)}) collective-permute-start(f32[13,36,2]{2,1,0:T(8,128)S(1)} %get-tuple-element.179), channel_id=1, source_target_pairs={{1,0},{2,1},{3,2},{5,4},{6,5},{7,6},{9,8},{10,9},{11,10},{13,12},{... | collective-permute-start | bytes 11240 | tf_op jit(solution)/shard_map/ppermute | solution.py:20
  45.5 8.2 %collective-permute-start.6 = (f32[13,40,4]{2,1,0:T(8,128)S(1)}, f32[13,40,4]{2,1,0:T(8,128)S(1)}, u32[]{:S(2)}, u32[]{:S(2)}) collective-permute-start(f32[13,40,4]{2,1,0:T(8,128)S(1)} %get-tuple-element.182), channel_id=1, source_target_pairs={{0,1},{1,2},{2,3},{4,5},{5,6},{6,7},{8,9},{9,10},{10,11},{12,13},{... | collective-permute-start | bytes 24968 | tf_op jit(solution)/shard_map/ppermute | solution.py:17
  52.2 3.4 collective-permute-start.7
  305.6 180.2 %copy-start.1 = (f32[39,64]{1,0:T(8,128)S(1)}, f32[39,64]{1,0:T(8,128)}, u32[]{:S(2)}) copy-start(f32[39,64]{1,0:T(8,128)} %param.12) | copy-start | bytes 29956
Sparse Core Ops, SparseCore 0:
  324.9 159.1 reduce-scatter.1
where the time goes:
time: 494 us; the launch traced here: 493 us
  waiting for transfers between devices  165 us (33%)
  matrix products  147 us (30%)
  other arithmetic  109 us (22%)
  local copies, waits for them, and re-layouts  34.6 us (7%)
  starting transfers between devices  22.8 us (5%)
  between operations  13.7 us (3%)
    reduce_scatter x1, waiting for transfers between devices, body(): lax.psum_scatter(ordered, ('row', 'col'), scatter_dimension=0, tiled=True)  159 us
    dot_general x8, matrix products, accumulate(): jnp.einsum('kp,fbp->fkb', block_hot, weights, preferred_element_type=jnp....  146 us
    div x8, other arithmetic, tent_weights(): (clamped[:, None, :] - centres[:, :-1, None]) / bin_gaps[:, :, None]  91.9 us
    another operation x2, local copies, waits for them, and re-layouts, body(): whole_term.reshape(row_devices, feature_share, NODES, CLASSES, col_device...  19.1 us
    ppermute x4, starting transfers between devices, with_halo(): lax.ppermute(lax.slice_in_dim(block, block.shape[dim] - width, None, axis...  17.4 us
  transfers between devices with their start and end apart: 9, of which 3 were waited for; matrix products, arithmetic and copies ran while one was open for 4% of the time, Pallas kernels for 0%

commit v1 on v0

v1 whole, which is shorter than its diff:
```python
import functools

import jax
import jax.numpy as jnp
from jax import lax
from jax.experimental import pallas as pl
from jax.experimental.pallas import tpu as pltpu
from jax.sharding import PartitionSpec as P

FEAT = 64
BINS = 256
CLASSES = 40
NODES = 2
PAIRS = NODES * CLASSES
LANES = 128
MESH_ID = pl.DeviceIdType.MESH
VMEM = pl.BlockSpec(memory_space=pltpu.VMEM)
SMEM = pl.BlockSpec(memory_space=pltpu.SMEM)

DIRECTIONS = [(dr, dc) for dr in (-1, 0, 1) for dc in (-1, 0, 1) if (dr, dc) != (0, 0)]


def halo_kernel(rows, cols, bands_ref, out_ref, send_sem, recv_sem):
    height = bands_ref.shape[1]
    r = lax.axis_index("row")
    c = lax.axis_index("col")

    def inside(dr, dc):
        return (r + dr >= 0) & (r + dr < rows) & (c + dc >= 0) & (c + dc < cols)

    def row_span(d, far):
        if d == 0:
            return (0, height) if not far else (8, height)
        if d > 0:
            return (height - 8, 8) if not far else (0, 8)
        return (0, 8) if not far else (height + 8, 8)

    def copy_for(index):
        dr, dc = DIRECTIONS[index]
        from_row, count = row_span(dr, False)
        to_row, _ = row_span(dr, True)
        return pltpu.make_async_remote_copy(
            src_ref=bands_ref.at[:, pl.ds(from_row, count), :],
            dst_ref=out_ref.at[:, pl.ds(to_row, count), pl.ds((1 - dc) * LANES, LANES)],
            send_sem=send_sem.at[index],
            recv_sem=recv_sem.at[index],
            device_id=(r + dr, c + dc),
            device_id_type=MESH_ID,
        )

    barrier = pltpu.get_barrier_semaphore()
    depth = out_ref.shape[0]
    for dr, dc in DIRECTIONS:
        to_row, count = row_span(-dr, True)

        @pl.when(jnp.logical_not(inside(dr, dc)))
        def _():
            lane = (1 + dc) * LANES
            out_ref[:, to_row : to_row + count, lane : lane + LANES] = jnp.zeros(
                (depth, count, LANES), jnp.float32
            )

    for dr, dc in DIRECTIONS:

        @pl.when(inside(dr, dc))
        def _():
            pl.semaphore_signal(barrier, inc=1, device_id=(r + dr, c + dc), device_id_type=MESH_ID)

    tall = jnp.where(r > 0, 1, 0) + jnp.where(r < rows - 1, 1, 0) + 1
    wide = jnp.where(c > 0, 1, 0) + jnp.where(c < cols - 1, 1, 0) + 1
    pl.semaphore_wait(barrier, tall * wide - 1)

    for index, (dr, dc) in enumerate(DIRECTIONS):

        @pl.when(inside(dr, dc))
        def _():
            copy_for(index).start()

    out_ref[:, 8 : 8 + height, LANES : 2 * LANES] = bands_ref[...]
    for index, (dr, dc) in enumerate(DIRECTIONS):

        @pl.when(inside(dr, dc))
        def _():
            copy_for(index).wait_send()

        @pl.when(inside(-dr, -dc))
        def _():
            copy_for(index).wait_recv()


def exchange_halo(bands, rows, cols):
    depth, height, width = bands.shape
    return pl.pallas_call(
        functools.partial(halo_kernel, rows, cols),
        out_shape=jax.ShapeDtypeStruct((depth, height + 16, 3 * LANES), jnp.float32),
        in_specs=[VMEM],
        out_specs=VMEM,
        scratch_shapes=[pltpu.SemaphoreType.DMA((8,)), pltpu.SemaphoreType.DMA((8,))],
        compiler_params=pltpu.CompilerParams(
            collective_id=0, has_side_effects=True, vmem_limit_bytes=16 << 20
        ),
        name="halo",
    )(bands)


def feature_kernel(padded_ref, near_ref, far_ref, mix_ref, out_ref, shifted, stack):
    depth, tall, _ = padded_ref.shape
    height = tall - 16
    lane = lax.broadcasted_iota(jnp.int32, (height + 8, LANES), 1)

    def one_band(b, carry):
        left = padded_ref[b, 4 : 12 + height, 0:LANES]
        middle = padded_ref[b, 4 : 12 + height, LANES : 2 * LANES]
        right = padded_ref[b, 4 : 12 + height, 2 * LANES : 3 * LANES]
        for col_off in range(9):
            s = col_off - 4
            if s == 0:
                window = middle
            elif s > 0:
                window = pltpu.roll(jnp.where(lane >= s, middle, right), LANES - s, 1)
            else:
                window = pltpu.roll(jnp.where(lane < LANES + s, middle, left), -s, 1)
            shifted[col_off] = window
        small = jnp.zeros((height, LANES), jnp.float32)
        large = jnp.zeros((height, LANES), jnp.float32)
        for row_off in range(9):
            for col_off in range(9):
                window = shifted[col_off, row_off : row_off + height, :]
                large = large + far_ref[b, row_off * 9 + col_off] * window
                if 2 <= row_off <= 6 and 2 <= col_off <= 6:
                    small = small + near_ref[b, (row_off - 2) * 5 + col_off - 2] * window
        stack[b] = middle[4 : 4 + height, :]
        stack[depth + b] = small
        stack[2 * depth + b] = large
        return carry

    lax.fori_loop(0, depth, one_band, 0)
    for i in range(height):
        channels = stack[:, i, :]
        out_ref[:, i * LANES : (i + 1) * LANES] = jnp.dot(
            mix_ref[...],
            channels,
            precision=lax.Precision.HIGHEST,
            preferred_element_type=jnp.float32,
        )


def compute_features(padded, kern_small, kern_large, mix_rows):
    depth, tall, _ = padded.shape
    height = tall - 16
    return pl.pallas_call(
        feature_kernel,
        out_shape=jax.ShapeDtypeStruct((FEAT, height * LANES), jnp.float32),
        in_specs=[VMEM, SMEM, SMEM, VMEM],
        out_specs=VMEM,
        scratch_shapes=[
            pltpu.VMEM((9, height + 8, LANES), jnp.float32),
            pltpu.VMEM((3 * depth, height, LANES), jnp.float32),
        ],
        compiler_params=pltpu.CompilerParams(vmem_limit_bytes=24 << 20),
        name="features",
    )(padded, kern_small.reshape(depth, 25), kern_large.reshape(depth, 81), mix_rows)


def swap_kernel(inner, cols, feats_ref, code_ref, feats_out, code_out, send_sem, recv_sem, own_sem):
    r = lax.axis_index("row")
    c = lax.axis_index("col")
    base = r - lax.rem(r, inner)
    me = lax.rem(r, inner) * cols + c
    group = inner * cols

    def peer(step):
        other = lax.rem(me + step, group)
        return other, (base + other // cols, lax.rem(other, cols))

    barrier = pltpu.get_barrier_semaphore()
    for step in range(1, group):
        pl.semaphore_signal(barrier, inc=1, device_id=peer(step)[1], device_id_type=MESH_ID)
    pl.semaphore_wait(barrier, group - 1)
    own = pltpu.make_async_copy(feats_ref.at[me], feats_out.at[me], own_sem.at[0])
    own.start()
    own_code = pltpu.make_async_copy(code_ref, code_out.at[me], own_sem.at[1])
    own_code.start()
    copies = []
    for step in range(1, group):
        other, device = peer(step)
        copies.append(
            pltpu.make_async_remote_copy(
                src_ref=feats_ref.at[other],
                dst_ref=feats_out.at[me],
                send_sem=send_sem.at[0, step],
                recv_sem=recv_sem.at[0, step],
                device_id=device,
                device_id_type=MESH_ID,
            )
        )
        copies.append(
            pltpu.make_async_remote_copy(
                src_ref=code_ref,
                dst_ref=code_out.at[me],
                send_sem=send_sem.at[1, step],
                recv_sem=recv_sem.at[1, step],
                device_id=device,
                device_id_type=MESH_ID,
            )
        )
    for copy in copies:
        copy.start()
    own.wait()
    own_code.wait()
    for copy in copies:
        copy.wait()


def swap_features(feats, code, inner, cols):
    group = inner * cols
    share, pixels = feats.shape[0] // group, feats.shape[1]
    return pl.pallas_call(
        functools.partial(swap_kernel, inner, cols),
        out_shape=[
            jax.ShapeDtypeStruct((group, share, pixels), jnp.float32),
            jax.ShapeDtypeStruct((group,) + code.shape, jnp.int32),
        ],
        in_specs=[VMEM, VMEM],
        out_specs=[VMEM, VMEM],
        scratch_shapes=[
            pltpu.SemaphoreType.DMA((2, group)),
            pltpu.SemaphoreType.DMA((2, group)),
            pltpu.SemaphoreType.DMA((2,)),
        ],
        compiler_params=pltpu.CompilerParams(
            collective_id=1, has_side_effects=True, vmem_limit_bytes=16 << 20
        ),
        name="swap",
    )(feats.reshape(group, share, pixels), code)


CHUNK_ROWS = 8


def hist_kernel(feats_ref, code_ref, centres_ref, out_ref, even_pos, odd_pos, even_w, odd_w):
    sources, share, pixels = feats_ref.shape
    low_table = centres_ref[:, 0:LANES]
    high_table = centres_ref[:, LANES : 2 * LANES]
    first = jnp.broadcast_to(low_table[:, 0:1], (share, LANES))
    centre = jnp.broadcast_to(high_table[:, 0:1], (share, LANES))
    last = jnp.broadcast_to(high_table[:, LANES - 1 : LANES], (share, LANES))
    span = CHUNK_ROWS * LANES
    chunks = pixels // span
    bin_rows = lax.broadcasted_iota(jnp.int32, (LANES, LANES), 0).astype(jnp.float32)
    bin_rows = bin_rows.astype(jnp.bfloat16)
    pair_rows = lax.broadcasted_iota(jnp.int32, (PAIRS, LANES), 0)
    zero = jnp.zeros((LANES, LANES), jnp.bfloat16)
    out_ref[...] = jnp.zeros_like(out_ref)

    def spread(row):
        block = jnp.broadcast_to(row, (16, LANES)).astype(jnp.bfloat16)
        return jnp.concatenate([block] * (LANES // 16), axis=0)

    def one_chunk(step, carry):
        source = step // chunks
        start = pl.multiple_of(lax.rem(step, chunks) * span, span)
        row_start = lax.rem(step, chunks) * CHUNK_ROWS
        for i in range(CHUNK_ROWS):
            v = feats_ref[source, :, pl.ds(start + i * LANES, LANES)]
            v = jnp.minimum(jnp.maximum(v, first), last)
            upper_half = v >= centre
            below = jnp.where(upper_half, centre, first)
            above = jnp.where(upper_half, last, centre)
            pos = jnp.zeros((share, LANES), jnp.int32)
            for bit in (64, 32, 16, 8, 4, 2, 1):
                cand = pos + bit
                probe = jnp.where(
                    upper_half,
                    jnp.take_along_axis(high_table, cand, axis=1, mode="promise_in_bounds"),
                    jnp.take_along_axis(low_table, cand, axis=1, mode="promise_in_bounds"),
                )
                right = v >= probe
                if bit == 1:
                    right = right & (probe < last)
                pos = jnp.where(right, cand, pos)
                below = jnp.where(right, probe, below)
                above = jnp.where(right, above, probe)
            lower = jnp.where(upper_half, pos + LANES, pos)
            gap = above - below
            fall = jnp.minimum(jnp.maximum((above - v) / gap, 0.0), 1.0)
            rise = jnp.minimum(jnp.maximum((v - below) / gap, 0.0), 1.0)
            is_odd = (lower & 1) == 1
            half = lower >> 1
            at = slice(i * LANES, (i + 1) * LANES)
            odd_pos[:, at] = half.astype(jnp.float32)
            even_pos[:, at] = jnp.where(is_odd, half + 1, half).astype(jnp.float32)
            even_w[:, at] = jnp.where(is_odd, rise, fall)
            odd_w[:, at] = jnp.where(is_odd, fall, rise)
        hot = []
        for i in range(CHUNK_ROWS):
            code = jnp.broadcast_to(code_ref[source, pl.ds(row_start + i, 1), :], (PAIRS, LANES))
            hot.append(jnp.where(code == pair_rows, 1.0, 0.0).astype(jnp.bfloat16))
        hot = jnp.concatenate(hot, axis=1)
        for f in range(share):
            columns = []
            for i in range(CHUNK_ROWS):
                at = slice(i * LANES, (i + 1) * LANES)
                even = jnp.where(
                    bin_rows == spread(even_pos[f : f + 1, at]), spread(even_w[f : f + 1, at]), zero
                )
                odd = jnp.where(
                    bin_rows == spread(odd_pos[f : f + 1, at]), spread(odd_w[f : f + 1, at]), zero
                )
                columns.append(jnp.concatenate([even, odd], axis=0))
            tent = jnp.concatenate(columns, axis=1)
            out_ref[f] += lax.dot_general(
                hot, tent, (((1,), (1,)), ((), ())), preferred_element_type=jnp.float32
            )
        return carry

    lax.fori_loop(0, sources * chunks, one_chunk, 0)


def histograms(feats, code, centres):
    sources, share, pixels = feats.shape
    span = CHUNK_ROWS * LANES
    return pl.pallas_call(
        hist_kernel,
        out_shape=jax.ShapeDtypeStruct((share, PAIRS, BINS), jnp.float32),
        in_specs=[VMEM, VMEM, VMEM],
        out_specs=VMEM,
        scratch_shapes=[pltpu.VMEM((share, span), jnp.float32)] * 4,
        compiler_params=pltpu.CompilerParams(vmem_limit_bytes=32 << 20),
        name="histograms",
    )(feats, code, centres)


def reduce_kernel(outer, inner, cols, scale, hist_ref, out_ref, parts, packed, slabs, send_a, recv_a, send_b, recv_b):
    r = lax.axis_index("row")
    c = lax.axis_index("col")
    z = r // inner
    y = lax.rem(r, inner)

    def along_z(step):
        other = lax.rem(z + step, outer)
        return other, (other * inner + y, c)

    def along_c(step):
        other = lax.rem(c + step, cols)
        return other, (r, other)

    barrier = pltpu.get_barrier_semaphore()
    for step in range(1, outer):
        pl.semaphore_signal(barrier, inc=1, device_id=along_z(step)[1], device_id_type=MESH_ID)
    for step in range(1, cols):
        pl.semaphore_signal(barrier, inc=1, device_id=along_c(step)[1], device_id_type=MESH_ID)
    pl.semaphore_wait(barrier, outer + cols - 2)

    copies = []
    for step in range(1, outer):
        other, device = along_z(step)
        copies.append(
            pltpu.make_async_remote_copy(
                src_ref=hist_ref.at[other],
                dst_ref=parts.at[step],
                send_sem=send_a.at[step],
                recv_sem=recv_a.at[step],
                device_id=device,
                device_id_type=MESH_ID,
            )
        )
        copies[-1].start()
    for copy in copies:
        copy.wait()

    lane = lax.broadcasted_iota(jnp.int32, (8, LANES), 1)
    odd_lane = (lane & 1) == 1
    second = lane >= LANES // 2
    pick = (lane & (LANES // 2 - 1)) >> 1

    def gather(table, index):
        return jnp.take_along_axis(table, index, axis=1, mode="promise_in_bounds")

    def one_block(block, carry):
        row = pl.multiple_of(block * 8, 8)
        total = []
        for k in range(2):
            halves = []
            for side in range(2):
                at = pl.ds(side * LANES, LANES)
                value = hist_ref[z, k, pl.ds(row, 8), at]
                for step in range(1, outer):
                    value = value + parts[step, k, pl.ds(row, 8), at]
                halves.append(value * scale)
            total.append(halves)
        for dest in range(cols):
            index = pick + dest * (LANES // cols)
            by_k = [
                jnp.where(odd_lane, gather(total[k][1], index), gather(total[k][0], index))
                for k in range(2)
            ]
            packed[dest, pl.ds(row, 8), :] = jnp.where(second, by_k[1], by_k[0])
        return carry

    lax.fori_loop(0, PAIRS // 8, one_block, 0)

    copies = []
    for step in range(1, cols):
        other, device = along_c(step)
        copies.append(
            pltpu.make_async_remote_copy(
                src_ref=packed.at[other],
                dst_ref=slabs.at[c],
                send_sem=send_b.at[step],
                recv_sem=recv_b.at[step],
                device_id=device,
                device_id_type=MESH_ID,
            )
        )
        copies[-1].start()
    slabs[c] = packed[c]
    for copy in copies:
        copy.wait()
    for source in range(cols):
        out_ref[2 * source] = slabs[source, :, 0 : LANES // 2]
        out_ref[2 * source + 1] = slabs[source, :, LANES // 2 : LANES]


def reduce_histograms(hist, outer, inner, cols, scale):
    return pl.pallas_call(
        functools.partial(reduce_kernel, outer, inner, cols, scale),
        out_shape=jax.ShapeDtypeStruct((2 * cols, PAIRS, LANES // 2), jnp.float32),
        in_specs=[VMEM],
        out_specs=VMEM,
        scratch_shapes=[
            pltpu.VMEM((outer, 2, PAIRS, BINS), jnp.float32),
            pltpu.VMEM((cols, PAIRS, LANES), jnp.float32),
            pltpu.VMEM((cols, PAIRS, LANES), jnp.float32),
            pltpu.SemaphoreType.DMA((outer,)),
            pltpu.SemaphoreType.DMA((outer,)),
            pltpu.SemaphoreType.DMA((cols,)),
            pltpu.SemaphoreType.DMA((cols,)),
        ],
        compiler_params=pltpu.CompilerParams(
            collective_id=2, has_side_effects=True, vmem_limit_bytes=24 << 20
        ),
        name="reduce",
    )(hist.reshape(outer, 2, PAIRS, BINS))


def body(rows, cols, bands, kern_small, kern_large, mix_weight, node_ids, labels, edges):
    band_count, tile_height, tile_width = bands.shape
    pixels = tile_height * tile_width
    scale = float(NODES * CLASSES * BINS) / float(pixels * rows * cols)
    centres = edges.astype(jnp.float32) / 1024.0
    code = node_ids * CLASSES + labels
    padded = exchange_halo(bands, rows, cols)
    share = FEAT // rows
    inner = 2
    outer = rows // inner
    if rows % inner == 0 and share == 2 * cols and cols * (BINS // cols) == BINS and BINS // cols == 64:
        mix_rows = mix_weight.T.reshape(outer, inner, cols, 2, 3 * band_count)
        mix_rows = mix_rows.transpose(1, 2, 0, 3, 4).reshape(FEAT, 3 * band_count)
        own = centres.reshape(outer, inner, cols, 2, BINS)
        own = own[:, lax.axis_index("row") % inner, lax.axis_index("col")].reshape(2 * outer, BINS)
        feats = compute_features(padded, kern_small, kern_large, mix_rows)
        feats, code = swap_features(feats, code, inner, cols)
        hist = histograms(feats, code, own)
        summed = reduce_histograms(hist, outer, inner, cols, scale)
        return summed.reshape(share, NODES, CLASSES, BINS // cols)
    feats = compute_features(padded, kern_small, kern_large, mix_weight.T)
    hist = jnp.concatenate(
        [
            histograms(feats[None, i : i + 8], code[None], centres[i : i + 8])
            for i in range(0, FEAT, 8)
        ]
    )
    hist = hist.reshape(FEAT, PAIRS, 2, BINS // 2).swapaxes(2, 3)
    ordered = hist.reshape(rows, share, NODES, CLASSES, cols, BINS // cols)
    ordered = ordered.transpose(0, 4, 1, 2, 3, 5).reshape(
        rows * cols * share, NODES, CLASSES, BINS // cols
    )
    summed = lax.psum_scatter(ordered, ("row", "col"), scatter_dimension=0, tiled=True)
    return summed * scale


def solution(mesh):
    return jax.shard_map(
        functools.partial(body, mesh.shape["row"], mesh.shape["col"]),
        mesh=mesh,
        in_specs=(P(None, "row", "col"), P(), P(), P(), P("row", "col"), P("row", "col"), P()),
        out_specs=P("row", None, None, "col"),
        check_vma=False,
    )
```

time: 494 us -> 125 us (0.25)
  waiting for transfers between devices: 165 us -> 0 us
  matrix products: 147 us -> 0 us
  Pallas kernels: 0 us -> 120 us
  other arithmetic: 109 us -> 0.01 us
  local copies, waits for them, and re-layouts: 34.6 us -> 2.69 us
  starting transfers between devices: 22.8 us -> 0 us
  between operations: 13.7 us -> 0.16 us
    reduce_scatter x1 -> x0, waiting for transfers between devices: 159 us -> none  [body(): lax.psum_scatter(ordered, ('row', 'col'), scatter_dimension=0, tiled=True)]
    dot_general x9 -> x0, matrix products: 147 us -> none  [the longest x8 146 us: accumulate(): jnp.einsum('kp,fbp->fkb', block_hot, weights, preferred_element_type=jnp....]
    pallas_call x0 -> x5, Pallas kernels: none -> 120 us  [the longest x1 67.7 us: histograms(): pl.pallas_call(hist_kernel, out_shape=jax.ShapeDtypeStruct((share, PAIRS,...]
    div x9 -> x1, other arithmetic: 91.9 us -> 0.01 us  [body(): centres = edges.astype(jnp.float32) / 1024.0]
    ppermute x8 -> x0, starting transfers between devices: 22.8 us -> none  [the longest x4 17.4 us: with_halo(): lax.ppermute(lax.slice_in_dim(block, block.shape[dim] - width, None, axis...]
    another operation x2 -> x1, local copies, waits for them, and re-layouts: 19.1 us -> 0.01 us  [body(): own[:, lax.axis_index('row') % inner, lax.axis_index('col')]]
    slice x34 -> x0, local copies, waits for them, and re-layouts: 11.1 us -> none  [the longest x5 7.72 us: stencil(): running = running + kernel[:, row_off, col_off][:, None, None] * window]
    add x3 -> x1, other arithmetic: 10.4 us -> 0.01 us  [body(): code = node_ids * CLASSES + labels]
  transfers between devices with their start and end apart: 9 -> 0, of which waited for: 3 -> 0; matrix products, arithmetic and copies ran while one was open for 4% -> 0% of each run, Pallas kernels for 0% -> 0%
where the time goes in v1:
time: 125 us; the launch traced here: 123 us
  Pallas kernels  120 us (96%)
  local copies, waits for them, and re-layouts  2.69 us (2%)
    pallas_call x1, Pallas kernels, histograms(): pl.pallas_call(hist_kernel, out_shape=jax.ShapeDtypeStruct((share, PAIRS,...  67.7 us
    pallas_call x1, Pallas kernels, reduce_histograms(): pl.pallas_call(functools.partial(reduce_kernel, outer, inner, cols, scale...  21.4 us
    pallas_call x1, Pallas kernels, swap_features(): pl.pallas_call(functools.partial(swap_kernel, inner, cols), out_shape=[ja...  16.2 us
    pallas_call x1, Pallas kernels, exchange_halo(): pl.pallas_call(functools.partial(halo_kernel, rows, cols), out_shape=jax....  9.66 us
    pallas_call x1, Pallas kernels, compute_features(): pl.pallas_call(feature_kernel, out_shape=jax.ShapeDtypeStruct((FEAT, heig...  5.27 us

profile of v1, /device:TPU:0, one launch (start us, length us, event | category | flops | bytes accessed | tf_op | source)
XLA Modules:
  0.0 123.1 jit_solution(12193575087291362593)
XLA Ops:
  0.0 0.0 copy-start
  0.0 0.9 copy-done
  0.9 0.0 copy-start.3
  0.9 0.0 copy-start.1
  0.9 9.7 %halo.1.padded_ref = f32[13,48,384]{2,1,0:T(8,128)S(1)} custom-call(f32[13,32,128]{2,1,0:T(8,128)S(1)} %copy-done), custom_call_target="tpu_custom_call" | custom-call | tf_op jit(solution)/shard_map/halo/pallas_call | solution.py:93
  10.6 0.0 copy-done.3
  10.6 0.1 copy.15.near_ref
  10.7 0.0 copy-done.1
  10.7 0.0 copy-start.4
  10.8 0.1 reshape.25.far_ref
  10.8 0.6 copy-done.4
  11.5 0.1 copy.13
  11.6 0.0 copy-start.5
  11.6 0.0 copy-start.6
  11.6 5.3 %features.1 = f32[64,4096]{1,0:T(8,128)S(1)} custom-call(f32[13,48,384]{2,1,0:T(8,128)S(1)} %halo.1.padded_ref, f32[13,25]{1,0:T(8,128)S(1)} %copy.15.near_ref, f32[13,81]{1,0:T(8,128)S(1)} %reshape.25.far_ref, f32[64,39]{1,0:T(8,128)S(1)} %bitcast.18), custom_call_target="tpu_custom_call" | custom-call | tf_op jit(solution)/shard_map/features/pallas_call | solution.py:151
  16.9 0.0 copy-done.5
  16.9 0.0 copy-done.6
  16.9 0.0 copy-start.2
  16.9 16.2 %swap.1 = (f32[8,8,4096]{2,1,0:T(8,128)S(1)}, s32[8,32,128]{2,1,0:T(8,128)S(1)}) custom-call(f32[8,8,4096]{2,1,0:T(8,128)S(1)} %bitcast.15, s32[32,128]{1,0:T(8,128)S(1)} %multiply_add_fusion.code_ref), custom_call_target="tpu_custom_call" | custom-call | tf_op jit(solution)/shard_map/swap/pallas_call | solution.py:218
  33.1 0.0 copy-done.2
  33.3 67.7 %histograms.1 = f32[8,80,256]{2,1,0:T(8,128)S(1)} custom-call(f32[8,8,4096]{2,1,0:T(8,128)S(1)} %get-tuple-element.7.feats_ref, s32[8,32,128]{2,1,0:T(8,128)S(1)} %get-tuple-element.8.code_ref, f32[8,256]{1,0:T(8,128)S(1)} %reshape_squeeze.3.centres_ref), custom_call_target="tpu_custom_call" | custom-call | tf_op jit(solution)/shard_map/histograms/pallas_call | solution.py:323
  101.0 21.4 %reduce.1 = f32[8,80,64]{2,1,0:T(8,128)S(1)} custom-call(f32[4,2,80,256]{3,2,1,0:T(8,128)S(1)} %bitcast.16), custom_call_target="tpu_custom_call" | custom-call | tf_op jit(solution)/shard_map/reduce/pallas_call | solution.py:426
  122.3 0.7 copy.19
  (8 shorter events, 0.1 us)
Async XLA Ops:
  0.0 0.9 copy-start
  0.9 9.7 %copy-start.3 = (f32[13,5,5]{0,2,1:T(8,128)S(1)}, f32[13,5,5]{0,2,1:T(8,128)}, u32[]{:S(2)}) copy-start(f32[13,5,5]{0,2,1:T(8,128)} %param.8) | copy-start | bytes 3904
  0.9 9.8 %copy-start.1 = (f32[13,9,9]{2,0,1:T(8,128)S(1)}, f32[13,9,9]{2,0,1:T(8,128)}, u32[]{:S(2)}) copy-start(f32[13,9,9]{2,0,1:T(8,128)} %param.9) | copy-start | bytes 12640
  10.7 0.7 copy-start.4
  11.6 5.3 %copy-start.5 = (s32[32,128]{1,0:T(8,128)S(1)}, s32[32,128]{1,0:T(8,128)}, u32[]{:S(2)}) copy-start(s32[32,128]{1,0:T(8,128)} %param.12) | copy-start | bytes 49156
  11.6 5.3 %copy-start.6 = (s32[32,128]{1,0:T(8,128)S(1)}, s32[32,128]{1,0:T(8,128)}, u32[]{:S(2)}) copy-start(s32[32,128]{1,0:T(8,128)} %param.11) | copy-start | bytes 49156
  16.9 16.2 %copy-start.2 = (s32[64,256]{1,0:T(8,128)S(1)}, s32[64,256]{1,0:T(8,128)}, u32[]{:S(2)}) copy-start(s32[64,256]{1,0:T(8,128)} %param.13) | copy-start | bytes 196612

commit v2 on v1

--- a/solution.py
+++ b/solution.py
@@ -162,173 +162,206 @@
     )(padded, kern_small.reshape(depth, 25), kern_large.reshape(depth, 81), mix_rows)
 
 
-def swap_kernel(inner, cols, feats_ref, code_ref, feats_out, code_out, send_sem, recv_sem, own_sem):
-    r = lax.axis_index("row")
-    c = lax.axis_index("col")
-    base = r - lax.rem(r, inner)
-    me = lax.rem(r, inner) * cols + c
-    group = inner * cols
-
-    def peer(step):
-        other = lax.rem(me + step, group)
-        return other, (base + other // cols, lax.rem(other, cols))
-
-    barrier = pltpu.get_barrier_semaphore()
-    for step in range(1, group):
-        pl.semaphore_signal(barrier, inc=1, device_id=peer(step)[1], device_id_type=MESH_ID)
-    pl.semaphore_wait(barrier, group - 1)
-    own = pltpu.make_async_copy(feats_ref.at[me], feats_out.at[me], own_sem.at[0])
-    own.start()
-    own_code = pltpu.make_async_copy(code_ref, code_out.at[me], own_sem.at[1])
-    own_code.start()
-    copies = []
-    for step in range(1, group):
-        other, device = peer(step)
-        copies.append(
-            pltpu.make_async_remote_copy(
-                src_ref=feats_ref.at[other],
-                dst_ref=feats_out.at[me],
-                send_sem=send_sem.at[0, step],
-                recv_sem=recv_sem.at[0, step],
-                device_id=device,
-                device_id_type=MESH_ID,
-            )
-        )
-        copies.append(
-            pltpu.make_async_remote_copy(
-                src_ref=code_ref,
-                dst_ref=code_out.at[me],
-                send_sem=send_sem.at[1, step],
-                recv_sem=recv_sem.at[1, step],
-                device_id=device,
-                device_id_type=MESH_ID,
-            )
-        )
-    for copy in copies:
-        copy.start()
-    own.wait()
-    own_code.wait()
-    for copy in copies:
-        copy.wait()
-
-
-def swap_features(feats, code, inner, cols):
-    group = inner * cols
-    share, pixels = feats.shape[0] // group, feats.shape[1]
-    return pl.pallas_call(
-        functools.partial(swap_kernel, inner, cols),
-        out_shape=[
-            jax.ShapeDtypeStruct((group, share, pixels), jnp.float32),
-            jax.ShapeDtypeStruct((group,) + code.shape, jnp.int32),
-        ],
-        in_specs=[VMEM, VMEM],
-        out_specs=[VMEM, VMEM],
-        scratch_shapes=[
-            pltpu.SemaphoreType.DMA((2, group)),
-            pltpu.SemaphoreType.DMA((2, group)),
-            pltpu.SemaphoreType.DMA((2,)),
-        ],
-        compiler_params=pltpu.CompilerParams(
-            collective_id=1, has_side_effects=True, vmem_limit_bytes=16 << 20
-        ),
-        name="swap",
-    )(feats.reshape(group, share, pixels), code)
-
-
-CHUNK_ROWS = 8
-
-
-def hist_kernel(feats_ref, code_ref, centres_ref, out_ref, even_pos, odd_pos, even_w, odd_w):
-    sources, share, pixels = feats_ref.shape
-    low_table = centres_ref[:, 0:LANES]
-    high_table = centres_ref[:, LANES : 2 * LANES]
-    first = jnp.broadcast_to(low_table[:, 0:1], (share, LANES))
-    centre = jnp.broadcast_to(high_table[:, 0:1], (share, LANES))
-    last = jnp.broadcast_to(high_table[:, LANES - 1 : LANES], (share, LANES))
-    span = CHUNK_ROWS * LANES
-    chunks = pixels // span
-    bin_rows = lax.broadcasted_iota(jnp.int32, (LANES, LANES), 0).astype(jnp.float32)
-    bin_rows = bin_rows.astype(jnp.bfloat16)
-    pair_rows = lax.broadcasted_iota(jnp.int32, (PAIRS, LANES), 0)
+def accumulate(feats, code_of, centres_ref, pos_ref, w_ref, hot_ref, acc_ref):
+    share, pixels = feats.shape
+    height = pixels // LANES
+    even_table = centres_ref[:, 0:LANES]
+    odd_table = centres_ref[:, LANES : 2 * LANES]
+
+    def edge(table, i):
+        return jnp.broadcast_to(table[:, i : i + 1], (share, LANES))
+
+    first, last = edge(even_table, 0), edge(odd_table, LANES - 1)
+    at64, at32, at96 = [edge(even_table, i) for i in (64, 32, 96)]
+    at16, at48, at80, at112 = [edge(even_table, i) for i in (16, 48, 80, 112)]
+    for i in range(height):
+        at = slice(i * LANES, (i + 1) * LANES)
+        v = jnp.minimum(jnp.maximum(feats[:, at], first), last)
+        right1 = v >= at64
+        probe = jnp.where(right1, at96, at32)
+        below = jnp.where(right1, at64, first)
+        above = jnp.where(right1, last, at64)
+        pos = jnp.where(right1, 64, 0)
+        right2 = v >= probe
+        below = jnp.where(right2, probe, below)
+        above = jnp.where(right2, above, probe)
+        pos = jnp.where(right2, pos + 32, pos)
+        probe = jnp.where(right1, jnp.where(right2, at112, at80), jnp.where(right2, at48, at16))
+        right3 = v >= probe
+        below = jnp.where(right3, probe, below)
+        above = jnp.where(right3, above, probe)
+        pos = jnp.where(right3, pos + 16, pos)
+        for bit in (8, 4, 2, 1):
+            cand = pos + bit
+            probe = jnp.take_along_axis(even_table, cand, axis=1, mode="promise_in_bounds")
+            right = v >= probe
+            pos = jnp.where(right, cand, pos)
+            below = jnp.where(right, probe, below)
+            above = jnp.where(right, above, probe)
+        probe = jnp.take_along_axis(odd_table, pos, axis=1, mode="promise_in_bounds")
+        right = (v >= probe) & (probe < last)
+        below = jnp.where(right, probe, below)
+        above = jnp.where(right, above, probe)
+        gap = above - below
+        fall = jnp.minimum(jnp.maximum((above - v) / gap, 0.0), 1.0)
+        rise = jnp.minimum(jnp.maximum((v - below) / gap, 0.0), 1.0)
+        pos_ref[0, :, at] = jnp.where(right, pos + 1, pos).astype(jnp.float32)
+        pos_ref[1, :, at] = pos.astype(jnp.float32)
+        w_ref[0, :, at] = jnp.where(right, rise, fall)
+        w_ref[1, :, at] = jnp.where(right, fall, rise)
+    rows = lax.broadcasted_iota(jnp.int32, (LANES, LANES), 0)
+    for i in range(height):
+        code = jnp.broadcast_to(code_of(i), (LANES, LANES))
+        hot_ref[:, i * LANES : (i + 1) * LANES] = jnp.where(code == rows, 1.0, 0.0).astype(
+            jnp.bfloat16
+        )
+    bin_rows = rows.astype(jnp.float32).astype(jnp.bfloat16)
     zero = jnp.zeros((LANES, LANES), jnp.bfloat16)
-    out_ref[...] = jnp.zeros_like(out_ref)
 
     def spread(row):
         block = jnp.broadcast_to(row, (16, LANES)).astype(jnp.bfloat16)
         return jnp.concatenate([block] * (LANES // 16), axis=0)
 
-    def one_chunk(step, carry):
-        source = step // chunks
-        start = pl.multiple_of(lax.rem(step, chunks) * span, span)
-        row_start = lax.rem(step, chunks) * CHUNK_ROWS
-        for i in range(CHUNK_ROWS):
-            v = feats_ref[source, :, pl.ds(start + i * LANES, LANES)]
-            v = jnp.minimum(jnp.maximum(v, first), last)
-            upper_half = v >= centre
-            below = jnp.where(upper_half, centre, first)
-            above = jnp.where(upper_half, last, centre)
-            pos = jnp.zeros((share, LANES), jnp.int32)
-            for bit in (64, 32, 16, 8, 4, 2, 1):
-                cand = pos + bit
-                probe = jnp.where(
-                    upper_half,
-                    jnp.take_along_axis(high_table, cand, axis=1, mode="promise_in_bounds"),
-                    jnp.take_along_axis(low_table, cand, axis=1, mode="promise_in_bounds"),
-                )
-                right = v >= probe
-                if bit == 1:
-                    right = right & (probe < last)
-                pos = jnp.where(right, cand, pos)
-                below = jnp.where(right, probe, below)
-                above = jnp.where(right, above, probe)
-            lower = jnp.where(upper_half, pos + LANES, pos)
-            gap = above - below
-            fall = jnp.minimum(jnp.maximum((above - v) / gap, 0.0), 1.0)
-            rise = jnp.minimum(jnp.maximum((v - below) / gap, 0.0), 1.0)
-            is_odd = (lower & 1) == 1
-            half = lower >> 1
-            at = slice(i * LANES, (i + 1) * LANES)
-            odd_pos[:, at] = half.astype(jnp.float32)
-            even_pos[:, at] = jnp.where(is_odd, half + 1, half).astype(jnp.float32)
-            even_w[:, at] = jnp.where(is_odd, rise, fall)
-            odd_w[:, at] = jnp.where(is_odd, fall, rise)
-        hot = []
-        for i in range(CHUNK_ROWS):
-            code = jnp.broadcast_to(code_ref[source, pl.ds(row_start + i, 1), :], (PAIRS, LANES))
-            hot.append(jnp.where(code == pair_rows, 1.0, 0.0).astype(jnp.bfloat16))
-        hot = jnp.concatenate(hot, axis=1)
-        for f in range(share):
-            columns = []
-            for i in range(CHUNK_ROWS):
+    hot = hot_ref[...]
+    for f in range(share):
+        for side in range(2):
+            tent = []
+            for i in range(height):
                 at = slice(i * LANES, (i + 1) * LANES)
-                even = jnp.where(
-                    bin_rows == spread(even_pos[f : f + 1, at]), spread(even_w[f : f + 1, at]), zero
-                )
-                odd = jnp.where(
-                    bin_rows == spread(odd_pos[f : f + 1, at]), spread(odd_w[f : f + 1, at]), zero
-                )
-                columns.append(jnp.concatenate([even, odd], axis=0))
-            tent = jnp.concatenate(columns, axis=1)
-            out_ref[f] += lax.dot_general(
-                hot, tent, (((1,), (1,)), ((), ())), preferred_element_type=jnp.float32
+                hit = bin_rows == spread(pos_ref[side, f : f + 1, at])
+                tent.append(jnp.where(hit, spread(w_ref[side, f : f + 1, at]), zero))
+            acc_ref[f, side] += lax.dot_general(
+                jnp.concatenate(tent, axis=1),
+                hot,
+                (((1,), (1,)), ((), ())),
+                preferred_element_type=jnp.float32,
             )
-        return carry
-
-    lax.fori_loop(0, sources * chunks, one_chunk, 0)
+
+
+def write_histograms(acc_ref, out_ref):
+    for f in range(out_ref.shape[0]):
+        for side in range(2):
+            out_ref[f, :, side * LANES : (side + 1) * LANES] = acc_ref[f, side].T[:PAIRS]
+
+
+def hist_kernel(feats_ref, code_ref, centres_ref, out_ref, pos_ref, w_ref, hot_ref, acc_ref):
+    acc_ref[...] = jnp.zeros_like(acc_ref)
+    accumulate(
+        feats_ref, lambda i: code_ref[i : i + 1, :], centres_ref, pos_ref, w_ref, hot_ref, acc_ref
+    )
+    write_histograms(acc_ref, out_ref)
+
+
+def work_buffers(share, pixels):
+    return [
+        pltpu.VMEM((2, share, pixels), jnp.float32),
+        pltpu.VMEM((2, share, pixels), jnp.float32),
+        pltpu.VMEM((LANES, pixels), jnp.bfloat16),
+        pltpu.VMEM((share, 2, LANES, LANES), jnp.float32),
+    ]
+
+
+def split_bins(centres):
+    return jnp.concatenate([centres[:, 0::2], centres[:, 1::2]], axis=1)
 
 
 def histograms(feats, code, centres):
-    sources, share, pixels = feats.shape
-    span = CHUNK_ROWS * LANES
+    share, pixels = feats.shape
     return pl.pallas_call(
         hist_kernel,
         out_shape=jax.ShapeDtypeStruct((share, PAIRS, BINS), jnp.float32),
         in_specs=[VMEM, VMEM, VMEM],
         out_specs=VMEM,
-        scratch_shapes=[pltpu.VMEM((share, span), jnp.float32)] * 4,
-        compiler_params=pltpu.CompilerParams(vmem_limit_bytes=32 << 20),
+        scratch_shapes=work_buffers(share, pixels),
+        compiler_params=pltpu.CompilerParams(vmem_limit_bytes=40 << 20),
         name="histograms",
-    )(feats, code, centres)
+    )(feats, code, split_bins(centres))
+
+
+def swap_kernel(
+    feats_ref, code_ref, centres_ref, out_ref,
+    got, got_code, pos_ref, w_ref, hot_ref, acc_ref, send_sem, recv_sem,
+):
+    r = lax.axis_index("row")
+    c = lax.axis_index("col")
+    y, x, core = lax.rem(r, 2), c // 2, lax.rem(c, 2)
+
+    def peer(step):
+        other_y = lax.rem(y + step // 4, 2)
+        other_c = lax.rem(x + lax.rem(step // 2, 2), 2) * 2 + lax.rem(core + lax.rem(step, 2), 2)
+        return other_y * 4 + other_c, (r - y + other_y, other_c)
+
+    def copies(step):
+        other, device = peer(step)
+        return (
+            pltpu.make_async_remote_copy(
+                src_ref=feats_ref.at[other],
+                dst_ref=got.at[step],
+                send_sem=send_sem.at[0, step],
+                recv_sem=recv_sem.at[0, step],
+                device_id=device,
+                device_id_type=MESH_ID,
+            ),
+            pltpu.make_async_remote_copy(
+                src_ref=code_ref,
+                dst_ref=got_code.at[step],
+                send_sem=send_sem.at[1, step],
+                recv_sem=recv_sem.at[1, step],
+                device_id=device,
+                device_id_type=MESH_ID,
+            ),
+        )
+
+    barrier = pltpu.get_barrier_semaphore()
+    for step in range(1, 8):
+        pl.semaphore_signal(barrier, inc=1, device_id=peer(jnp.int32(step))[1], device_id_type=MESH_ID)
+    pl.semaphore_wait(barrier, 7)
+    for step in range(1, 8):
+        for copy in copies(jnp.int32(step)):
+            copy.start()
+    got[0] = feats_ref[y * 4 + c]
+    got_code[0] = code_ref[...]
+    acc_ref[...] = jnp.zeros_like(acc_ref)
+
+    def one_source(step, carry):
+        @pl.when(step > 0)
+        def _():
+            for copy in copies(step):
+                copy.wait_recv()
+
+        accumulate(
+            got.at[step],
+            lambda i: got_code[step, i : i + 1, :],
+            centres_ref, pos_ref, w_ref, hot_ref, acc_ref,
+        )
+        return carry
+
+    lax.fori_loop(0, 8, one_source, 0)
+    for step in range(1, 8):
+        for copy in copies(jnp.int32(step)):
+            copy.wait_send()
+    write_histograms(acc_ref, out_ref)
+
+
+def swap_histograms(feats, code, centres):
+    share, pixels = feats.shape[0] // 8, feats.shape[1]
+    return pl.pallas_call(
+        swap_kernel,
+        out_shape=jax.ShapeDtypeStruct((share, PAIRS, BINS), jnp.float32),
+        in_specs=[VMEM, VMEM, VMEM],
+        out_specs=VMEM,
+        scratch_shapes=[
+            pltpu.VMEM((8, share, pixels), jnp.float32),
+            pltpu.VMEM((8,) + code.shape, jnp.int32),
+            *work_buffers(share, pixels),
+            pltpu.SemaphoreType.DMA((2, 8)),
+            pltpu.SemaphoreType.DMA((2, 8)),
+        ],
+        compiler_params=pltpu.CompilerParams(
+            collective_id=1, has_side_effects=True, vmem_limit_bytes=40 << 20
+        ),
+        name="swap_histograms",
+    )(feats.reshape(8, share, pixels), code, split_bins(centres))
 
 
 def reduce_kernel(outer, inner, cols, scale, hist_ref, out_ref, parts, packed, slabs, send_a, recv_a, send_b, recv_b):
@@ -454,20 +487,19 @@
     share = FEAT // rows
     inner = 2
     outer = rows // inner
-    if rows % inner == 0 and share == 2 * cols and cols * (BINS // cols) == BINS and BINS // cols == 64:
+    if rows % inner == 0 and cols == 4 and share == 8:
         mix_rows = mix_weight.T.reshape(outer, inner, cols, 2, 3 * band_count)
         mix_rows = mix_rows.transpose(1, 2, 0, 3, 4).reshape(FEAT, 3 * band_count)
         own = centres.reshape(outer, inner, cols, 2, BINS)
         own = own[:, lax.axis_index("row") % inner, lax.axis_index("col")].reshape(2 * outer, BINS)
         feats = compute_features(padded, kern_small, kern_large, mix_rows)
-        feats, code = swap_features(feats, code, inner, cols)
-        hist = histograms(feats, code, own)
+        hist = swap_histograms(feats, code, own)
         summed = reduce_histograms(hist, outer, inner, cols, scale)
         return summed.reshape(share, NODES, CLASSES, BINS // cols)
     feats = compute_features(padded, kern_small, kern_large, mix_weight.T)
     hist = jnp.concatenate(
         [
-            histograms(feats[None, i : i + 8], code[None], centres[i : i + 8])
+            histograms(feats[i : i + 8], code, centres[i : i + 8])
             for i in range(0, FEAT, 8)
         ]
     )

time: 125 us -> 86.8 us (0.69)
  Pallas kernels: 120 us -> 82.2 us
    pallas_call x2 -> x1, Pallas kernels: 83.9 us -> 47.5 us  [swap_histograms(): pl.pallas_call(swap_kernel, out_shape=jax.ShapeDtypeStruct((share, PAIRS,...]
    pallas_call x1, Pallas kernels: 21.4 us -> 19.9 us  [reduce_histograms(): pl.pallas_call(functools.partial(reduce_kernel, outer, inner, cols, scale...]
where the time goes in v2:
time: 86.8 us; the launch traced here: 85.5 us
  Pallas kernels  82.2 us (95%)
  local copies, waits for them, and re-layouts  3.09 us (4%)
    pallas_call x1, Pallas kernels, swap_histograms(): pl.pallas_call(swap_kernel, out_shape=jax.ShapeDtypeStruct((share, PAIRS,...  47.5 us
    pallas_call x1, Pallas kernels, reduce_histograms(): pl.pallas_call(functools.partial(reduce_kernel, outer, inner, cols, scale...  19.9 us
    pallas_call x1, Pallas kernels, exchange_halo(): pl.pallas_call(functools.partial(halo_kernel, rows, cols), out_shape=jax....  9.66 us
    pallas_call x1, Pallas kernels, compute_features(): pl.pallas_call(feature_kernel, out_shape=jax.ShapeDtypeStruct((FEAT, heig...  5.26 us
    unnamed x18, local copies, waits for them, and re-layouts  2.44 us

profile of v2, /device:TPU:0, one launch (start us, length us, event | category | flops | bytes accessed | tf_op | source)
XLA Modules:
  0.0 85.5 jit_solution(4840783476565135121)
XLA Ops:
  0.0 0.0 copy-start
  0.0 0.9 %copy-done = f32[13,32,128]{2,1,0:T(8,128)S(1)} copy-done((f32[13,32,128]{2,1,0:T(8,128)S(1)}, f32[13,32,128]{2,1,0:T(8,128)}, u32[]{:S(2)}) %copy-start) | copy-done | bytes 213016
  0.9 0.0 copy-start.3
  0.9 0.0 copy-start.1
  0.9 9.7 %halo.1.padded_ref = f32[13,48,384]{2,1,0:T(8,128)S(1)} custom-call(f32[13,32,128]{2,1,0:T(8,128)S(1)} %copy-done), custom_call_target="tpu_custom_call" | custom-call | tf_op jit(solution)/shard_map/halo/pallas_call | solution.py:93
  10.6 0.0 copy-done.3
  10.6 0.1 copy.15.near_ref
  10.7 0.0 copy-done.1
  10.7 0.0 copy-start.4
  10.8 0.1 reshape.25.far_ref
  10.8 0.6 copy-done.4
  11.5 0.1 copy.13
  11.6 0.0 copy-start.5
  11.6 0.0 copy-start.6
  11.6 0.0 copy-start.2
  11.6 5.3 %features.1 = f32[64,4096]{1,0:T(8,128)S(1)} custom-call(f32[13,48,384]{2,1,0:T(8,128)S(1)} %halo.1.padded_ref, f32[13,25]{1,0:T(8,128)S(1)} %copy.15.near_ref, f32[13,81]{1,0:T(8,128)S(1)} %reshape.25.far_ref, f32[64,39]{1,0:T(8,128)S(1)} %bitcast.18), custom_call_target="tpu_custom_call" | custom-call | tf_op jit(solution)/shard_map/features/pallas_call | solution.py:151
  16.9 0.0 copy-done.5
  16.9 0.0 copy-done.6
  16.9 0.0 copy-done.2
  17.0 0.2 slice.7
  17.2 0.2 slice.6
  17.5 47.5 %swap_histograms.1 = f32[8,80,256]{2,1,0:T(8,128)S(1)} custom-call(f32[8,8,4096]{2,1,0:T(8,128)S(1)} %bitcast.15, s32[32,128]{1,0:T(8,128)S(1)} %multiply_add_fusion.code_ref, f32[8,256]{1,0:T(8,128)S(1)} %pad_maximum_fusion.centres_ref), custom_call_target="tpu_custom_call" | custom-call | tf_op jit(solution)/shard_map/swap_histograms/pallas_call | solution.py:348
  64.9 19.9 %reduce.1 = f32[8,80,64]{2,1,0:T(8,128)S(1)} custom-call(f32[4,2,80,256]{3,2,1,0:T(8,128)S(1)} %bitcast.16), custom_call_target="tpu_custom_call" | custom-call | tf_op jit(solution)/shard_map/reduce/pallas_call | solution.py:459
  84.8 0.7 copy.19
  (9 shorter events, 0.1 us)
Async XLA Ops:
  0.0 0.9 %copy-start = (f32[13,32,128]{2,1,0:T(8,128)S(1)}, f32[13,32,128]{2,1,0:T(8,128)}, u32[]{:S(2)}) copy-start(f32[13,32,128]{2,1,0:T(8,128)} %bands_ref.1) | copy-start | bytes 638980
  0.9 9.7 %copy-start.3 = (f32[13,5,5]{0,2,1:T(8,128)S(1)}, f32[13,5,5]{0,2,1:T(8,128)}, u32[]{:S(2)}) copy-start(f32[13,5,5]{0,2,1:T(8,128)} %param.8) | copy-start | bytes 3904
  0.9 9.8 %copy-start.1 = (f32[13,9,9]{2,0,1:T(8,128)S(1)}, f32[13,9,9]{2,0,1:T(8,128)}, u32[]{:S(2)}) copy-start(f32[13,9,9]{2,0,1:T(8,128)} %param.9) | copy-start | bytes 12640
  10.7 0.7 copy-start.4
  11.6 5.3 %copy-start.5 = (s32[32,128]{1,0:T(8,128)S(1)}, s32[32,128]{1,0:T(8,128)}, u32[]{:S(2)}) copy-start(s32[32,128]{1,0:T(8,128)} %param.12) | copy-start | bytes 49156
  11.6 5.3 %copy-start.6 = (s32[32,128]{1,0:T(8,128)S(1)}, s32[32,128]{1,0:T(8,128)}, u32[]{:S(2)}) copy-start(s32[32,128]{1,0:T(8,128)} %param.11) | copy-start | bytes 49156
  11.6 5.3 %copy-start.2 = (s32[64,256]{1,0:T(8,128)S(1)}, s32[64,256]{1,0:T(8,128)}, u32[]{:S(2)}) copy-start(s32[64,256]{1,0:T(8,128)} %param.13) | copy-start | bytes 196612

commit v3 on v2

--- a/solution.py
+++ b/solution.py
@@ -162,7 +162,7 @@
     )(padded, kern_small.reshape(depth, 25), kern_large.reshape(depth, 81), mix_rows)
 
 
-def accumulate(feats, code_of, centres_ref, pos_ref, w_ref, hot_ref, acc_ref):
+def locate(feats, code_of, centres_ref, pos_ref, w_ref, hot_ref):
     share, pixels = feats.shape
     height = pixels // LANES
     even_table = centres_ref[:, 0:LANES]
@@ -215,6 +215,11 @@
         hot_ref[:, i * LANES : (i + 1) * LANES] = jnp.where(code == rows, 1.0, 0.0).astype(
             jnp.bfloat16
         )
+
+
+def accumulate(features, pos_ref, w_ref, hot_ref, acc_ref):
+    height = hot_ref.shape[1] // LANES
+    rows = lax.broadcasted_iota(jnp.int32, (LANES, LANES), 0)
     bin_rows = rows.astype(jnp.float32).astype(jnp.bfloat16)
     zero = jnp.zeros((LANES, LANES), jnp.bfloat16)
 
@@ -223,7 +228,7 @@
         return jnp.concatenate([block] * (LANES // 16), axis=0)
 
     hot = hot_ref[...]
-    for f in range(share):
+    for f in features:
         for side in range(2):
             tent = []
             for i in range(height):
@@ -246,9 +251,8 @@
 
 def hist_kernel(feats_ref, code_ref, centres_ref, out_ref, pos_ref, w_ref, hot_ref, acc_ref):
     acc_ref[...] = jnp.zeros_like(acc_ref)
-    accumulate(
-        feats_ref, lambda i: code_ref[i : i + 1, :], centres_ref, pos_ref, w_ref, hot_ref, acc_ref
-    )
+    locate(feats_ref, lambda i: code_ref[i : i + 1, :], centres_ref, pos_ref, w_ref, hot_ref)
+    accumulate(range(out_ref.shape[0]), pos_ref, w_ref, hot_ref, acc_ref)
     write_histograms(acc_ref, out_ref)
 
 
@@ -279,8 +283,9 @@
 
 
 def swap_kernel(
-    feats_ref, code_ref, centres_ref, out_ref,
-    got, got_code, pos_ref, w_ref, hot_ref, acc_ref, send_sem, recv_sem,
+    outer, cols, scale, feats_ref, code_ref, centres_ref, out_ref,
+    got, got_code, pos_ref, w_ref, hot_ref, acc_ref, hist, parts, packed, slabs,
+    send_sem, recv_sem, send_a, recv_a, send_b, recv_b,
 ):
     r = lax.axis_index("row")
     c = lax.axis_index("col")
@@ -312,10 +317,40 @@
             ),
         )
 
+    z = r // 2
+    half, odd = z // 2, lax.rem(z, 2)
+
+    def partial_copy(step):
+        to_odd = lax.rem(odd + step, 2)
+        if step < 2:
+            slot, other = to_odd, (1 - half) * 2 + to_odd
+        else:
+            to_odd = 1 - odd
+            slot, other = 2 + to_odd, half * 2 + to_odd
+        return pltpu.make_async_remote_copy(
+            src_ref=hist.at[slot],
+            dst_ref=parts.at[step],
+            send_sem=send_a.at[step],
+            recv_sem=recv_a.at[step],
+            device_id=(other * 2 + y, c),
+            device_id_type=MESH_ID,
+        )
+
+    def along_c(step):
+        other = lax.rem(c + step, cols)
+        return other, (r, other)
+
     barrier = pltpu.get_barrier_semaphore()
     for step in range(1, 8):
         pl.semaphore_signal(barrier, inc=1, device_id=peer(jnp.int32(step))[1], device_id_type=MESH_ID)
-    pl.semaphore_wait(barrier, 7)
+    for step in range(1, outer):
+        pl.semaphore_signal(
+            barrier,
+            inc=1,
+            device_id=(lax.rem(z + step, outer) * 2 + y, c),
+            device_id_type=MESH_ID,
+        )
+    pl.semaphore_wait(barrier, 7 + outer - 1)
     for step in range(1, 8):
         for copy in copies(jnp.int32(step)):
             copy.start()
@@ -323,83 +358,39 @@
     got_code[0] = code_ref[...]
     acc_ref[...] = jnp.zeros_like(acc_ref)
 
-    def one_source(step, carry):
+    def first_half(step, carry):
         @pl.when(step > 0)
         def _():
             for copy in copies(step):
                 copy.wait_recv()
 
-        accumulate(
-            got.at[step],
-            lambda i: got_code[step, i : i + 1, :],
-            centres_ref, pos_ref, w_ref, hot_ref, acc_ref,
-        )
+        views = (pos_ref.at[step], w_ref.at[step], hot_ref.at[step])
+        locate(got.at[step], lambda i: got_code[step, i : i + 1, :], centres_ref, *views)
+        accumulate(range(4), *views, acc_ref)
         return carry
 
-    lax.fori_loop(0, 8, one_source, 0)
+    def second_half(step, carry):
+        accumulate(range(4, 8), pos_ref.at[step], w_ref.at[step], hot_ref.at[step], acc_ref)
+        return carry
+
+    def write(features):
+        for f in features:
+            for side in range(2):
+                at = slice(side * LANES, (side + 1) * LANES)
+                hist[f // 2, f % 2, :, at] = acc_ref[f, side].T[:PAIRS]
+
+    lax.fori_loop(0, 8, first_half, 0)
+    write(range(4))
+    partials = [partial_copy(step) for step in range(3)]
+    partials[0].start()
+    partials[1].start()
+    lax.fori_loop(0, 8, second_half, 0)
+    write(range(4, 8))
+    partials[2].start()
     for step in range(1, 8):
         for copy in copies(jnp.int32(step)):
             copy.wait_send()
-    write_histograms(acc_ref, out_ref)
-
-
-def swap_histograms(feats, code, centres):
-    share, pixels = feats.shape[0] // 8, feats.shape[1]
-    return pl.pallas_call(
-        swap_kernel,
-        out_shape=jax.ShapeDtypeStruct((share, PAIRS, BINS), jnp.float32),
-        in_specs=[VMEM, VMEM, VMEM],
-        out_specs=VMEM,
-        scratch_shapes=[
-            pltpu.VMEM((8, share, pixels), jnp.float32),
-            pltpu.VMEM((8,) + code.shape, jnp.int32),
-            *work_buffers(share, pixels),
-            pltpu.SemaphoreType.DMA((2, 8)),
-            pltpu.SemaphoreType.DMA((2, 8)),
-        ],
-        compiler_params=pltpu.CompilerParams(
-            collective_id=1, has_side_effects=True, vmem_limit_bytes=40 << 20
-        ),
-        name="swap_histograms",
-    )(feats.reshape(8, share, pixels), code, split_bins(centres))
-
-
-def reduce_kernel(outer, inner, cols, scale, hist_ref, out_ref, parts, packed, slabs, send_a, recv_a, send_b, recv_b):
-    r = lax.axis_index("row")
-    c = lax.axis_index("col")
-    z = r // inner
-    y = lax.rem(r, inner)
-
-    def along_z(step):
-        other = lax.rem(z + step, outer)
-        return other, (other * inner + y, c)
-
-    def along_c(step):
-        other = lax.rem(c + step, cols)
-        return other, (r, other)
-
-    barrier = pltpu.get_barrier_semaphore()
-    for step in range(1, outer):
-        pl.semaphore_signal(barrier, inc=1, device_id=along_z(step)[1], device_id_type=MESH_ID)
-    for step in range(1, cols):
-        pl.semaphore_signal(barrier, inc=1, device_id=along_c(step)[1], device_id_type=MESH_ID)
-    pl.semaphore_wait(barrier, outer + cols - 2)
-
-    copies = []
-    for step in range(1, outer):
-        other, device = along_z(step)
-        copies.append(
-            pltpu.make_async_remote_copy(
-                src_ref=hist_ref.at[other],
-                dst_ref=parts.at[step],
-                send_sem=send_a.at[step],
-                recv_sem=recv_a.at[step],
-                device_id=device,
-                device_id_type=MESH_ID,
-            )
-        )
-        copies[-1].start()
-    for copy in copies:
+    for copy in partials:
         copy.wait()
 
     lane = lax.broadcasted_iota(jnp.int32, (8, LANES), 1)
@@ -417,8 +408,8 @@
             halves = []
             for side in range(2):
                 at = pl.ds(side * LANES, LANES)
-                value = hist_ref[z, k, pl.ds(row, 8), at]
-                for step in range(1, outer):
+                value = hist[2 + odd, k, pl.ds(row, 8), at]
+                for step in range(3):
                     value = value + parts[step, k, pl.ds(row, 8), at]
                 halves.append(value * scale)
             total.append(halves)
@@ -455,26 +446,36 @@
         out_ref[2 * source + 1] = slabs[source, :, LANES // 2 : LANES]
 
 
-def reduce_histograms(hist, outer, inner, cols, scale):
+def swap_histograms(feats, code, centres, outer, cols, scale):
+    share, pixels = feats.shape[0] // 8, feats.shape[1]
     return pl.pallas_call(
-        functools.partial(reduce_kernel, outer, inner, cols, scale),
+        functools.partial(swap_kernel, outer, cols, scale),
         out_shape=jax.ShapeDtypeStruct((2 * cols, PAIRS, LANES // 2), jnp.float32),
-        in_specs=[VMEM],
+        in_specs=[VMEM, VMEM, VMEM],
         out_specs=VMEM,
         scratch_shapes=[
+            pltpu.VMEM((8, share, pixels), jnp.float32),
+            pltpu.VMEM((8,) + code.shape, jnp.int32),
+            pltpu.VMEM((8, 2, share, pixels), jnp.float32),
+            pltpu.VMEM((8, 2, share, pixels), jnp.float32),
+            pltpu.VMEM((8, LANES, pixels), jnp.bfloat16),
+            pltpu.VMEM((share, 2, LANES, LANES), jnp.float32),
             pltpu.VMEM((outer, 2, PAIRS, BINS), jnp.float32),
+            pltpu.VMEM((3, 2, PAIRS, BINS), jnp.float32),
             pltpu.VMEM((cols, PAIRS, LANES), jnp.float32),
             pltpu.VMEM((cols, PAIRS, LANES), jnp.float32),
-            pltpu.SemaphoreType.DMA((outer,)),
-            pltpu.SemaphoreType.DMA((outer,)),
+            pltpu.SemaphoreType.DMA((2, 8)),
+            pltpu.SemaphoreType.DMA((2, 8)),
+            pltpu.SemaphoreType.DMA((3,)),
+            pltpu.SemaphoreType.DMA((3,)),
             pltpu.SemaphoreType.DMA((cols,)),
             pltpu.SemaphoreType.DMA((cols,)),
         ],
         compiler_params=pltpu.CompilerParams(
-            collective_id=2, has_side_effects=True, vmem_limit_bytes=24 << 20
+            collective_id=1, has_side_effects=True, vmem_limit_bytes=48 << 20
         ),
-        name="reduce",
-    )(hist.reshape(outer, 2, PAIRS, BINS))
+        name="swap_histograms",
+    )(feats.reshape(8, share, pixels), code, split_bins(centres))
 
 
 def body(rows, cols, bands, kern_small, kern_large, mix_weight, node_ids, labels, edges):
@@ -487,14 +488,16 @@
     share = FEAT // rows
     inner = 2
     outer = rows // inner
-    if rows % inner == 0 and cols == 4 and share == 8:
+    if rows == 8 and cols == 4 and share == 8:
+        far_half = lax.axis_index("row") < rows // 2
         mix_rows = mix_weight.T.reshape(outer, inner, cols, 2, 3 * band_count)
+        mix_rows = jnp.where(far_half, jnp.roll(mix_rows, 2, axis=0), mix_rows)
         mix_rows = mix_rows.transpose(1, 2, 0, 3, 4).reshape(FEAT, 3 * band_count)
         own = centres.reshape(outer, inner, cols, 2, BINS)
+        own = jnp.where(far_half, jnp.roll(own, 2, axis=0), own)
         own = own[:, lax.axis_index("row") % inner, lax.axis_index("col")].reshape(2 * outer, BINS)
         feats = compute_features(padded, kern_small, kern_large, mix_rows)
-        hist = swap_histograms(feats, code, own)
-        summed = reduce_histograms(hist, outer, inner, cols, scale)
+        summed = swap_histograms(feats, code, own, outer, cols, scale)
         return summed.reshape(share, NODES, CLASSES, BINS // cols)
     feats = compute_features(padded, kern_small, kern_large, mix_weight.T)
     hist = jnp.concatenate(

time: 86.8 us -> 78.4 us (0.903); the launches traced: 85.5 us -> 78.2 us
  Pallas kernels: 82.2 us -> 74.7 us
    pallas_call x2 -> x1, Pallas kernels: 67.3 us -> 59.8 us  [swap_histograms(): pl.pallas_call(functools.partial(swap_kernel, outer, cols, scale), out_sh...]
    unnamed x18 -> x17, local copies, waits for them, and re-layouts: 2.44 us -> 2.43 us
where the time goes in v3:
time: 78.4 us; the launch traced here: 78.2 us
  Pallas kernels  74.7 us (95%)
  local copies, waits for them, and re-layouts  3.16 us (4%)
    pallas_call x1, Pallas kernels, swap_histograms(): pl.pallas_call(functools.partial(swap_kernel, outer, cols, scale), out_sh...  59.8 us
    pallas_call x1, Pallas kernels, exchange_halo(): pl.pallas_call(functools.partial(halo_kernel, rows, cols), out_shape=jax....  9.66 us
    pallas_call x1, Pallas kernels, compute_features(): pl.pallas_call(feature_kernel, out_shape=jax.ShapeDtypeStruct((FEAT, heig...  5.26 us
    unnamed x17, local copies, waits for them, and re-layouts  2.43 us

profile of v3, /device:TPU:0, one launch (start us, length us, event | category | flops | bytes accessed | tf_op | source)
XLA Modules:
  0.0 78.2 jit_solution(8314521952021858450)
XLA Ops:
  0.0 0.0 copy-start
  0.0 0.9 %copy-done = f32[13,32,128]{2,1,0:T(8,128)S(1)} copy-done((f32[13,32,128]{2,1,0:T(8,128)S(1)}, f32[13,32,128]{2,1,0:T(8,128)}, u32[]{:S(2)}) %copy-start) | copy-done | bytes 213016
  0.9 0.0 copy-start.3
  0.9 0.0 copy-start.1
  0.9 9.7 %halo.1.padded_ref = f32[13,48,384]{2,1,0:T(8,128)S(1)} custom-call(f32[13,32,128]{2,1,0:T(8,128)S(1)} %copy-done), custom_call_target="tpu_custom_call" | custom-call | tf_op jit(solution)/shard_map/halo/pallas_call | solution.py:93
  10.6 0.0 copy-done.3
  10.6 0.1 copy.19.near_ref
  10.7 0.0 copy-done.1
  10.7 0.0 copy-start.4
  10.8 0.1 reshape.26.far_ref
  10.8 0.6 copy-done.4
  11.5 0.1 copy.17
  11.6 0.0 copy-start.5
  11.6 0.0 copy-start.6
  11.7 0.0 copy-start.2
  11.7 5.3 %features.1 = f32[64,4096]{1,0:T(8,128)S(1)} custom-call(f32[13,48,384]{2,1,0:T(8,128)S(1)} %halo.1.padded_ref, f32[13,25]{1,0:T(8,128)S(1)} %copy.19.near_ref, f32[13,81]{1,0:T(8,128)S(1)} %reshape.26.far_ref, f32[64,39]{1,0:T(8,128)S(1)} %bitcast.16), custom_call_target="tpu_custom_call" | custom-call | tf_op jit(solution)/shard_map/features/pallas_call | solution.py:151
  16.9 0.0 copy-done.5
  16.9 0.0 copy-done.6
  17.0 0.0 copy-done.2
  17.2 0.2 slice.43
  17.4 0.2 slice.42
  17.6 59.8 %swap_histograms.1 = f32[8,80,64]{2,1,0:T(8,128)S(1)} custom-call(f32[8,8,4096]{2,1,0:T(8,128)S(1)} %bitcast.14, s32[32,128]{1,0:T(8,128)S(1)} %multiply_add_fusion.code_ref, f32[8,256]{1,0:T(8,128)S(1)} %pad_maximum_fusion.1.centres_ref), custom_call_target="tpu_custom_call" | custom-call | tf_op jit(solution)/shard_map/swap_histograms/pallas_call | solution.py:451
  77.4 0.7 copy.29
  (16 shorter events, 0.2 us)
Async XLA Ops:
  0.0 0.9 %copy-start = (f32[13,32,128]{2,1,0:T(8,128)S(1)}, f32[13,32,128]{2,1,0:T(8,128)}, u32[]{:S(2)}) copy-start(f32[13,32,128]{2,1,0:T(8,128)} %bands_ref.1) | copy-start | bytes 638980
  0.9 9.7 %copy-start.3 = (f32[13,5,5]{0,2,1:T(8,128)S(1)}, f32[13,5,5]{0,2,1:T(8,128)}, u32[]{:S(2)}) copy-start(f32[13,5,5]{0,2,1:T(8,128)} %param.8) | copy-start | bytes 3904
  0.9 9.8 %copy-start.1 = (f32[13,9,9]{2,0,1:T(8,128)S(1)}, f32[13,9,9]{2,0,1:T(8,128)}, u32[]{:S(2)}) copy-start(f32[13,9,9]{2,0,1:T(8,128)} %param.9) | copy-start | bytes 12640
  10.7 0.7 copy-start.4
  11.6 5.3 %copy-start.5 = (s32[32,128]{1,0:T(8,128)S(1)}, s32[32,128]{1,0:T(8,128)}, u32[]{:S(2)}) copy-start(s32[32,128]{1,0:T(8,128)} %param.12) | copy-start | bytes 49156
  11.6 5.3 %copy-start.6 = (s32[32,128]{1,0:T(8,128)S(1)}, s32[32,128]{1,0:T(8,128)}, u32[]{:S(2)}) copy-start(s32[32,128]{1,0:T(8,128)} %param.11) | copy-start | bytes 49156
  11.7 5.3 %copy-start.2 = (s32[64,256]{1,0:T(8,128)S(1)}, s32[64,256]{1,0:T(8,128)}, u32[]{:S(2)}) copy-start(s32[64,256]{1,0:T(8,128)} %param.13) | copy-start | bytes 196612
